TPU v7x, 32 devices: a whole 2x2x4 slice. The times are simulated.
32 devices in a mesh: seq: 8 (over z, y), ch: 4 (over x, core).
Axes of the slice: x: 2, y: 2, z: 4, core: 2. Of those that a mesh axis runs over, the one named last changes fastest.
Arguments:
- stream: bfloat16 [2048, 1536], P('seq', 'ch'), may hold values from -6 to 6
- norm_gain: float32 [9, 1536], replicated, may hold values from 0.25 to 1.75
- conv_weight: bfloat16 [8, 3, 1536, 768], P(None, None, 'seq', 'ch'), may hold values from -0.09375 to 0.09375
- conv_bias: float32 [8, 768], P(None, 'ch'), may hold values from -3 to 3
- point_weight: bfloat16 [8, 768, 1536], P(None, 'seq', 'ch'), may hold values from -0.21875 to 0.21875
- point_bias: float32 [8, 1536], P(None, 'ch'), may hold values from -2 to 2
- head_weight: bfloat16 [1536, 3840], P('seq', 'ch'), may hold values from -0.15625 to 0.15625
- head_bias: float32 [3840], P('ch'), may hold values from -3 to 3
- exon_start: int32 [512], replicated, may hold values from 0 to 2016, as said below
- exon_length: int32 [512], replicated, may hold values from 1 to 32
- exon_transcript: int32 [512], replicated, may hold values from 0 to 63, as said below
- transcript_slot: int32 [64], replicated, may hold values from 0 to 63, each once
Outputs:
- transcript_cov: float32 [64, 3840], P('seq', 'ch')
Inputs may be any that keep to these rules, and one draw needn't show every extreme that they name: An exon of transcript t starts in bins t * 32 to t * 32 + 31, and exon_start[e] + exon_length[e] <= 2048. `exon_transcript`: never falls along the exons; every transcript has 1 to 15 exons, one exactly 15; transcripts 2 i and 2 i + 1 together have 2 * 8. `transcript_slot`: each row once.
All inputs are finite; a program needn't handle non-finite values.
Results may differ from a plain program's by a relative error of at most 0.00065.
Values may be sent and summed in bfloat16 or wider, within the bound.
A program may use at most 128 MiB of HBM per device.

v0:
```python
import jax
import jax.numpy as jnp
from jax import lax
from jax.experimental import pallas as pl
from jax.experimental.pallas import tpu as pltpu
from jax.sharding import PartitionSpec as P

LAYERS = 8


def padded(block, sides, width):
    for axis, dim in sides:
        count = lax.axis_size(axis)
        forward = [(i, i + 1) for i in range(count - 1)]
        backward = [(target, source) for source, target in forward]
        low = lax.ppermute(
            lax.slice_in_dim(block, block.shape[dim] - width, None, axis=dim), axis, forward
        )
        high = lax.ppermute(lax.slice_in_dim(block, 0, width, axis=dim), axis, backward)
        block = jnp.concatenate([low, block, high], axis=dim)
    return block


def rms_scaled(values, gain_row):
    wide = values.astype(jnp.float32)
    scale = lax.rsqrt(jnp.mean(wide * wide, axis=-1, keepdims=True) + 1e-06)
    return wide * scale * gain_row


def local_plain(
    stream,
    norm_gain,
    conv_weight,
    conv_bias,
    point_weight,
    point_bias,
    head_weight,
    head_bias,
    exon_start,
    exon_length,
    exon_transcript,
    transcript_slot,
):
    bin_rows = stream.shape[0]
    resid = stream
    for layer_idx in range(LAYERS):
        spread = 2**layer_idx
        rimmed = padded(resid, (("seq", 0),), spread)
        full_rows = lax.all_gather(rimmed, "ch", axis=1, tiled=True)
        act_rows = jax.nn.gelu(
            rms_scaled(full_rows, norm_gain[layer_idx]), approximate=False
        ).astype(jnp.bfloat16)
        tap_rows = jnp.stack(
            [
                act_rows[0:bin_rows],
                act_rows[spread : spread + bin_rows],
                act_rows[2 * spread : 2 * spread + bin_rows],
            ]
        )
        conv_sum = jnp.einsum(
            "kbc,kch->bh",
            tap_rows,
            lax.all_gather(conv_weight[layer_idx], "seq", axis=1, tiled=True),
            preferred_element_type=jnp.float32,
        )
        hidden = jax.nn.gelu(conv_sum + conv_bias[layer_idx], approximate=False).astype(
            jnp.bfloat16
        )
        hidden_all = lax.all_gather(hidden, "ch", axis=1, tiled=True)
        mixed = jnp.dot(
            hidden_all,
            lax.all_gather(point_weight[layer_idx], "seq", axis=0, tiled=True),
            preferred_element_type=jnp.float32,
        )
        resid = (resid.astype(jnp.float32) + mixed + point_bias[layer_idx]).astype(jnp.bfloat16)
    final_all = lax.all_gather(resid, "ch", axis=1, tiled=True)
    final_rows = rms_scaled(final_all, norm_gain[LAYERS]).astype(jnp.bfloat16)
    logits = jnp.dot(
        final_rows,
        lax.all_gather(head_weight, "seq", axis=0, tiled=True),
        preferred_element_type=jnp.float32,
    )
    coverage = jax.nn.softplus(logits + head_bias)
    seq_index = lax.axis_index("seq")
    bin_ids = seq_index * bin_rows + jnp.arange(bin_rows, dtype=jnp.int32)
    member = (
        (bin_ids[None, :] >= exon_start[:, None])
        & (bin_ids[None, :] < (exon_start + exon_length)[:, None])
    ).astype(jnp.bfloat16)
    owner_rows = transcript_slot[exon_transcript]
    select = (
        owner_rows[None, :] == jnp.arange(transcript_slot.shape[0], dtype=jnp.int32)[:, None]
    ).astype(jnp.bfloat16)
    counts = jnp.dot(select, member, preferred_element_type=jnp.float32)
    total = lax.psum_scatter(
        jnp.dot(counts, coverage, precision=lax.Precision.HIGHEST),
        "seq",
        scatter_dimension=0,
        tiled=True,
    )
    return jnp.log1p(total)


SEQ = 8
CHS = 4
HALF = 96
MESH = pl.DeviceIdType.MESH


def gelu(values):
    return 0.5 * values * (1.0 + lax.erf(values * 0.7071067811865476))


def tower_kernel(
    x_ref,
    gain_ref,
    conv_ref,
    conv_bias_ref,
    point_ref,
    point_bias_ref,
    head_ref,
    head_bias_ref,
    start_ref,
    length_ref,
    owner_ref,
    slot_ref,
    out_ref,
    weights,
    heads,
    streams,
    act,
    low_ext,
    high_ext,
    middle,
    hid,
    point,
    partial,
    landed,
    counts,
    conv_bias,
    head_bias,
    ring_send,
    ring_recv,
    x_send,
    x_recv,
    hid_send,
    hid_recv,
    halo_send,
    halo_recv,
    sum_send,
    sum_recv,
):
    seq = lax.axis_index("seq")
    ch = lax.axis_index("ch")
    rows = x_ref.shape[0]
    odd = seq % 2
    place = (1 - odd) * (seq // 2) + odd * (SEQ - 1 - seq // 2)

    def at_place(spot):
        spot = (spot + 2 * SEQ) % SEQ
        upper = spot // (SEQ // 2)
        return (1 - upper) * 2 * spot + upper * (2 * (SEQ - 1 - spot) + 1)

    ring_to = (at_place(place + 1), at_place(place - 1))
    sibling = ch + 1 - 2 * (ch % 2)
    across = (ch + 2) % CHS
    diagonal = (sibling + 2) % CHS

    barrier = pltpu.get_barrier_semaphore()
    for step in range(1, SEQ):
        pl.semaphore_signal(
            barrier, inc=1, device_id=((seq + step) % SEQ, ch), device_id_type=MESH
        )
    for peer in (sibling, across):
        pl.semaphore_signal(barrier, inc=1, device_id=(seq, peer), device_id_type=MESH)

    def pack(item):
        if item < LAYERS:
            last = point_ref[item, :, 256:384]
            strip = jnp.concatenate([last[:, 0:64], last[:, 64:128]], axis=0)
            own = weights.at[item, seq]
            own[:, 0:640] = jnp.concatenate(
                [conv_ref[item, 0], conv_ref[item, 1], conv_ref[item, 2], strip], axis=1
            )
            own[0:HALF, 640:768] = point_ref[item, :, 0:128]
            own[HALF : 2 * HALF, 640:768] = point_ref[item, :, 128:256]
        else:
            depth, tracks = head_ref.shape
            tail = tracks // 128 * 128
            own = heads.at[seq]
            own[:, tail:] = jnp.zeros((depth, heads.shape[2] - tail), jnp.bfloat16)
            own[:, 0:tracks] = head_ref[...]

    pack(0)
    streams[ch] = x_ref[...]
    pl.semaphore_wait(barrier, SEQ + 1)

    def reach(way, half):
        return 4 if way == half else 3

    def ring_copy(item, half, dist, way):
        origin = at_place(place - (dist - 1) if way == 0 else place + (dist - 1))
        part = pl.ds(half * HALF, HALF)
        if item < LAYERS:
            block = weights.at[item, origin, part]
        else:
            block = heads.at[origin, part]
        return pltpu.make_async_remote_copy(
            src_ref=block,
            dst_ref=block,
            send_sem=ring_send.at[way, item, half, dist - 1],
            recv_sem=ring_recv.at[way, item, half, dist - 1],
            device_id=(ring_to[way], ch),
            device_id_type=MESH,
        )

    def service(item, half, dist):
        for way in (0, 1):
            far = reach(way, half)
            if dist <= far:
                ring_copy(item, half, dist, way).wait_recv()
                if dist < far:
                    ring_copy(item, half, dist + 1, way).start()
        if dist == 2 and item < LAYERS:
            for way in (0, 1):
                ring_copy(item + 1, half, 1, way).start()

    def slot(item, number):
        if item > LAYERS:
            return
        if number < 6:
            service(item, number % 2, number // 2 + 1)
        else:
            service(item, 0, 4)
            service(item, 1, 4)

    for half in (0, 1):
        for way in (0, 1):
            ring_copy(0, half, 1, way).start()
    for item in range(1, LAYERS + 1):
        pack(item)

    slots = slot_ref.shape[1]
    bins = seq * rows + lax.broadcasted_iota(jnp.int32, (rows, start_ref.shape[1]), 0)
    member = (bins >= start_ref[...]) & (bins < start_ref[...] + length_ref[...])
    names = lax.broadcasted_iota(jnp.int32, (slots, owner_ref.shape[1]), 0)
    owned = lax.dot_general(
        jnp.where(names == owner_ref[...], 1.0, 0.0).astype(jnp.bfloat16),
        jnp.where(member, 1.0, 0.0).astype(jnp.bfloat16),
        (((1,), (1,)), ((), ())),
        preferred_element_type=jnp.float32,
    )
    order = lax.broadcasted_iota(jnp.int32, (slots, slots), 0) == slot_ref[...]
    counts[...] = jnp.dot(
        jnp.where(order, 1.0, 0.0).astype(jnp.bfloat16),
        owned.astype(jnp.bfloat16),
        preferred_element_type=jnp.float32,
    ).astype(jnp.bfloat16)
    conv_bias[...] = jnp.zeros_like(conv_bias)
    conv_bias[:, 0 : conv_bias_ref.shape[1]] = conv_bias_ref[...]
    head_bias[...] = jnp.zeros_like(head_bias)
    head_bias[:, 0 : head_bias_ref.shape[1]] = head_bias_ref[...]

    def spread_copies(buffer, sends, recvs, turn):
        def copy(block, peer, number):
            return pltpu.make_async_remote_copy(
                src_ref=buffer.at[block],
                dst_ref=buffer.at[block],
                send_sem=sends.at[turn, number],
                recv_sem=recvs.at[turn, number],
                device_id=(seq, peer),
                device_id_type=MESH,
            )

        return copy(ch, across, 0), copy(ch, sibling, 1), copy(across, sibling, 2)

    def norm_rows(turn, first, count, finish):
        tile = 32

        @pl.loop(0, count // tile)
        def _(index):
            part = pl.ds(pl.multiple_of(first + index * tile, tile), tile)
            blocks = [streams[block, part, :].astype(jnp.float32) for block in range(CHS)]
            width = blocks[0].shape[1]
            squares = sum(jnp.sum(b * b, axis=1, keepdims=True) for b in blocks)
            scale = lax.rsqrt(squares / (width * CHS) + 1e-06)
            for block in range(CHS):
                lanes = pl.ds(block * width, width)
                normed = blocks[block] * scale * gain_ref[pl.ds(turn, 1), lanes]
                act[part, lanes] = finish(normed).astype(jnp.bfloat16)

    def gather_stream(turn):
        first, second, third = spread_copies(streams, x_send, x_recv, turn)
        finish = gelu if turn < LAYERS else (lambda normed: normed)
        first.start()
        second.start()
        slot(turn, 3)
        first.wait_recv()
        third.start()
        slot(turn, 4)
        second.wait_recv()
        third.wait_recv()
        norm_rows(turn, 0, rows // 2, finish)
        slot(turn, 5)
        norm_rows(turn, rows // 2, rows // 2, finish)
        for copy in (first, second, third):
            copy.wait_send()
        slot(turn, 6)

    for number in (0, 1, 2):
        slot(0, number)

    for layer in range(LAYERS):
        spread = 2**layer
        rim = max(8, spread)
        pad = low_ext.shape[1] - rows
        gather_stream(layer)
        lows, highs = low_ext.at[layer % 2], high_ext.at[layer % 2]

        both = jnp.dot(
            act[...],
            weights[layer, :, :, 0:384].reshape(-1, 384),
            preferred_element_type=jnp.float32,
        )
        lows[pl.ds(pad, rows), :] = both[:, 0:256]
        middle[...] = both[:, 128:384]
        highs[pl.ds(0, rows), :] = jnp.dot(
            act[...],
            weights[layer, :, :, 384:640].reshape(-1, 256),
            preferred_element_type=jnp.float32,
        )

        up = pltpu.make_async_remote_copy(
            src_ref=lows.at[pl.ds(pad + rows - rim, rim)],
            dst_ref=lows.at[pl.ds(pad - rim, rim)],
            send_sem=halo_send.at[0, layer],
            recv_sem=halo_recv.at[0, layer],
            device_id=((seq + 1) % SEQ, ch),
            device_id_type=MESH,
        )
        down = pltpu.make_async_remote_copy(
            src_ref=highs.at[pl.ds(0, rim)],
            dst_ref=highs.at[pl.ds(rows, rim)],
            send_sem=halo_send.at[1, layer],
            recv_sem=halo_recv.at[1, layer],
            device_id=((seq + SEQ - 1) % SEQ, ch),
            device_id_type=MESH,
        )

        @pl.when(seq < SEQ - 1)
        def _():
            up.start()

        @pl.when(seq > 0)
        def _():
            down.start()

        slot(layer + 1, 0)

        for block in range(SEQ):
            here = pl.ds(block * HALF, HALF)
            point[here, 0:128] = weights[layer, block, 0:HALF, 640:768]
            point[here, 128:256] = weights[layer, block, HALF : 2 * HALF, 640:768]
            near = weights[layer, block, 0:HALF, 512:640].astype(jnp.float32)
            far = weights[layer, block, HALF : 2 * HALF, 512:640].astype(jnp.float32)
            lane = lax.broadcasted_iota(jnp.int32, near.shape, 1)
            point[here, 256:384] = jnp.where(
                lane < 64, pltpu.roll(near, 64, 1), far
            ).astype(jnp.bfloat16)

        @pl.when(seq > 0)
        def _():
            up.wait_recv()

        @pl.when(seq == 0)
        def _():
            lows[pl.ds(pad - rim, rim), :] = jnp.zeros((rim, 256), jnp.float32)

        @pl.when(seq < SEQ - 1)
        def _():
            down.wait_recv()

        @pl.when(seq == SEQ - 1)
        def _():
            highs[pl.ds(rows, rim), :] = jnp.zeros((rim, 256), jnp.float32)

        tile = 64
        for start in range(0, rows, tile):
            conv = (
                low_ext[layer % 2, pl.ds(pad - spread + start, tile), :]
                + pltpu.roll(middle[pl.ds(start, tile), :], 192, 1)
                + high_ext[layer % 2, pl.ds(spread + start, tile), :]
                + conv_bias[pl.ds(layer, 1), :]
            )
            hid[ch, pl.ds(start, tile), :] = gelu(conv).astype(jnp.bfloat16)

        first, second, third = spread_copies(hid, hid_send, hid_recv, layer)
        first.start()
        second.start()

        @pl.when(seq < SEQ - 1)
        def _():
            up.wait_send()

        @pl.when(seq > 0)
        def _():
            down.wait_send()

        slot(layer + 1, 1)
        first.wait_recv()
        third.start()
        slot(layer + 1, 2)
        second.wait_recv()
        third.wait_recv()
        mixed = streams[ch].astype(jnp.float32) + point_bias_ref[pl.ds(layer, 1), :]
        total = None
        for block in range(CHS):
            term = jnp.dot(
                hid[block, :, 0:192],
                point[block * 192 : (block + 1) * 192, :],
                preferred_element_type=jnp.float32,
            )
            total = term if total is None else total + term
        streams[ch] = (mixed + total).astype(jnp.bfloat16)
        for copy in (first, second, third):
            copy.wait_send()

    gather_stream(LAYERS)

    for start in range(0, heads.shape[2], 256):
        lanes = pl.ds(start, 256)
        logits = (
            jnp.dot(
                act[...],
                heads[:, :, start : start + 256].reshape(-1, 256),
                preferred_element_type=jnp.float32,
            )
            + head_bias[:, lanes]
        )
        cover = jnp.maximum(logits, 0.0) + jnp.log1p(jnp.exp(-jnp.abs(logits)))
        sums = None
        for _ in range(3):
            piece = cover.astype(jnp.bfloat16)
            term = jnp.dot(counts[...], piece, preferred_element_type=jnp.float32)
            sums = term if sums is None else sums + term
            cover = cover - piece.astype(jnp.float32)
        partial[:, :, lanes] = sums.reshape(SEQ, -1, 256)

    def sum_copy(step):
        target = (seq + step) % SEQ
        return pltpu.make_async_remote_copy(
            src_ref=partial.at[target],
            dst_ref=landed.at[step - 1],
            send_sem=sum_send.at[step - 1],
            recv_sem=sum_recv.at[step - 1],
            device_id=(target, ch),
            device_id_type=MESH,
        )

    for step in range(1, SEQ):
        sum_copy(step).start()
    for item in range(LAYERS + 1):
        for half in (0, 1):
            for way in (0, 1):
                for dist in range(1, reach(way, half) + 1):
                    ring_copy(item, half, dist, way).wait_send()
    result = partial[seq]
    for step in range(1, SEQ):
        sum_copy(step).wait_recv()
        result = result + landed[step - 1]
    out_ref[...] = jnp.log1p(result)[:, : out_ref.shape[1]]
    for step in range(1, SEQ):
        sum_copy(step).wait_send()


def local_kernel(
    stream,
    norm_gain,
    conv_weight,
    conv_bias,
    point_weight,
    point_bias,
    head_weight,
    head_bias,
    exon_start,
    exon_length,
    exon_transcript,
    transcript_slot,
):
    rows, width = stream.shape
    depth = conv_weight.shape[2]
    tracks = head_weight.shape[1]
    wide = -(-tracks // 256) * 256
    slots = transcript_slot.shape[0]
    vmem = pl.BlockSpec(memory_space=pltpu.VMEM)
    dma = pltpu.SemaphoreType.DMA
    return pl.pallas_call(
        tower_kernel,
        out_shape=jax.ShapeDtypeStruct((slots // SEQ, tracks), jnp.float32),
        in_specs=[vmem] * 12,
        out_specs=vmem,
        scratch_shapes=[
            pltpu.VMEM((LAYERS, SEQ, depth, 768), jnp.bfloat16),
            pltpu.VMEM((SEQ, depth, wide), jnp.bfloat16),
            pltpu.VMEM((CHS, rows, width), jnp.bfloat16),
            pltpu.VMEM((rows, CHS * width), jnp.bfloat16),
            pltpu.VMEM((2, rows + 128, 256), jnp.float32),
            pltpu.VMEM((2, rows + 128, 256), jnp.float32),
            pltpu.VMEM((rows, 256), jnp.float32),
            pltpu.VMEM((CHS, rows, 256), jnp.bfloat16),
            pltpu.VMEM((SEQ * HALF, width), jnp.bfloat16),
            pltpu.VMEM((SEQ, slots // SEQ, wide), jnp.float32),
            pltpu.VMEM((SEQ - 1, slots // SEQ, wide), jnp.float32),
            pltpu.VMEM((slots, rows), jnp.bfloat16),
            pltpu.VMEM((LAYERS, 256), jnp.float32),
            pltpu.VMEM((1, wide), jnp.float32),
            dma((2, LAYERS + 1, 2, 4)),
            dma((2, LAYERS + 1, 2, 4)),
            dma((LAYERS + 1, 3)),
            dma((LAYERS + 1, 3)),
            dma((LAYERS, 3)),
            dma((LAYERS, 3)),
            dma((2, LAYERS)),
            dma((2, LAYERS)),
            dma((SEQ - 1,)),
            dma((SEQ - 1,)),
        ],
        compiler_params=pltpu.CompilerParams(
            collective_id=0, has_side_effects=True, vmem_limit_bytes=56 * 2**20
        ),
        cost_estimate=pl.CostEstimate(
            flops=6_000_000_000, bytes_accessed=4_000_000, transcendentals=4_000_000
        ),
    )(
        stream,
        norm_gain,
        conv_weight,
        conv_bias,
        point_weight,
        point_bias,
        head_weight,
        head_bias[None, :],
        exon_start[None, :],
        exon_length[None, :],
        exon_transcript[None, :],
        transcript_slot[None, :],
    )


def local(*args):
    stream, conv_weight, point_weight = args[0], args[2], args[4]
    fits = (
        lax.axis_size("seq") == SEQ
        and lax.axis_size("ch") == CHS
        and stream.shape == (256, 384)
        and conv_weight.shape[2:] == (192, 192)
        and point_weight.shape[1:] == (HALF, 384)
        and args[11].shape[0] == 8 * SEQ
    )
    return local_kernel(*args) if fits else local_plain(*args)


def solution(mesh):
    placed = (
        P("seq", "ch"),
        P(),
        P(None, None, "seq", "ch"),
        P(None, "ch"),
        P(None, "seq", "ch"),
        P(None, "ch"),
        P("seq", "ch"),
        P("ch"),
        P(),
        P(),
        P(),
        P(),
    )
    return jax.shard_map(
        local, mesh=mesh, in_specs=placed, out_specs=P("seq", "ch"), check_vma=False
    )
```

profile of v0, /device:TPU:0, one launch (start us, length us, event | category | flops | bytes accessed | tf_op | source)
XLA Modules:
  0.0 255.6 jit_solution(10096256983835244374)
XLA Ops:
  0.0 254.2 %shard_map.118 = f32[8,960]{1,0:T(8,128)} custom-call(bf16[256,384]{1,0:T(8,128)(2,1)} %x_ref.1, f32[9,1536]{1,0:T(8,128)} %gain_ref.1, bf16[8,3,192,192]{3,2,1,0:T(8,128)(2,1)} %conv_ref.1, f32[8,192]{1,0:T(8,128)} %conv_bias_ref.1, bf16[8,96,384]{2,1,0:T(8,128)(2,1)} %point_ref.1, f32[8,384]{1,0:T(8,128)} %point_bias_ref.1, bf16[192,960]{1,0:T(8,128)(2,1)} %head_ref.1, ...), custom_call_target="tpu_custom_call" | custom-call | flops 6000000000 | bytes 4000000 | tf_op jit(solution)/shard_map/pallas_call | solution.py:497
  254.2 1.4 copy.14
where the time goes:
time: 256 us
  Pallas kernels  254 us (99%)
    pallas_call x1, Pallas kernels, local_kernel(): pl.pallas_call(tower_kernel, out_shape=jax.ShapeDtypeStruct((slots // SEQ...  254 us

commit v1 on v0

v1 whole, which is shorter than its diff:
```python
import jax
import jax.numpy as jnp
from jax import lax
from jax.experimental import pallas as pl
from jax.experimental.pallas import tpu as pltpu
from jax.sharding import PartitionSpec as P

LAYERS = 8


def padded(block, sides, width):
    for axis, dim in sides:
        count = lax.axis_size(axis)
        forward = [(i, i + 1) for i in range(count - 1)]
        backward = [(target, source) for source, target in forward]
        low = lax.ppermute(
            lax.slice_in_dim(block, block.shape[dim] - width, None, axis=dim), axis, forward
        )
        high = lax.ppermute(lax.slice_in_dim(block, 0, width, axis=dim), axis, backward)
        block = jnp.concatenate([low, block, high], axis=dim)
    return block


def rms_scaled(values, gain_row):
    wide = values.astype(jnp.float32)
    scale = lax.rsqrt(jnp.mean(wide * wide, axis=-1, keepdims=True) + 1e-06)
    return wide * scale * gain_row


def local_plain(
    stream,
    norm_gain,
    conv_weight,
    conv_bias,
    point_weight,
    point_bias,
    head_weight,
    head_bias,
    exon_start,
    exon_length,
    exon_transcript,
    transcript_slot,
):
    bin_rows = stream.shape[0]
    resid = stream
    for layer_idx in range(LAYERS):
        spread = 2**layer_idx
        rimmed = padded(resid, (("seq", 0),), spread)
        full_rows = lax.all_gather(rimmed, "ch", axis=1, tiled=True)
        act_rows = jax.nn.gelu(
            rms_scaled(full_rows, norm_gain[layer_idx]), approximate=False
        ).astype(jnp.bfloat16)
        tap_rows = jnp.stack(
            [
                act_rows[0:bin_rows],
                act_rows[spread : spread + bin_rows],
                act_rows[2 * spread : 2 * spread + bin_rows],
            ]
        )
        conv_sum = jnp.einsum(
            "kbc,kch->bh",
            tap_rows,
            lax.all_gather(conv_weight[layer_idx], "seq", axis=1, tiled=True),
            preferred_element_type=jnp.float32,
        )
        hidden = jax.nn.gelu(conv_sum + conv_bias[layer_idx], approximate=False).astype(
            jnp.bfloat16
        )
        hidden_all = lax.all_gather(hidden, "ch", axis=1, tiled=True)
        mixed = jnp.dot(
            hidden_all,
            lax.all_gather(point_weight[layer_idx], "seq", axis=0, tiled=True),
            preferred_element_type=jnp.float32,
        )
        resid = (resid.astype(jnp.float32) + mixed + point_bias[layer_idx]).astype(jnp.bfloat16)
    final_all = lax.all_gather(resid, "ch", axis=1, tiled=True)
    final_rows = rms_scaled(final_all, norm_gain[LAYERS]).astype(jnp.bfloat16)
    logits = jnp.dot(
        final_rows,
        lax.all_gather(head_weight, "seq", axis=0, tiled=True),
        preferred_element_type=jnp.float32,
    )
    coverage = jax.nn.softplus(logits + head_bias)
    seq_index = lax.axis_index("seq")
    bin_ids = seq_index * bin_rows + jnp.arange(bin_rows, dtype=jnp.int32)
    member = (
        (bin_ids[None, :] >= exon_start[:, None])
        & (bin_ids[None, :] < (exon_start + exon_length)[:, None])
    ).astype(jnp.bfloat16)
    owner_rows = transcript_slot[exon_transcript]
    select = (
        owner_rows[None, :] == jnp.arange(transcript_slot.shape[0], dtype=jnp.int32)[:, None]
    ).astype(jnp.bfloat16)
    counts = jnp.dot(select, member, preferred_element_type=jnp.float32)
    total = lax.psum_scatter(
        jnp.dot(counts, coverage, precision=lax.Precision.HIGHEST),
        "seq",
        scatter_dimension=0,
        tiled=True,
    )
    return jnp.log1p(total)


SEQ = 8
CHS = 4
BOTH = 0
START = 2
TILE = 32
CHUNKS = 960 // TILE
GROUP = 64
GROUPS = 960 // GROUP
IDLE = 3
EARLY = 192 // TILE
STEP = 448
CONV = 640
KEPT = 384
WIDE = 256
HEADW = 1024
MESH = pl.DeviceIdType.MESH
OFFSETS = (0, 1, -1, 2, -2, 3, -3, 4)


def gelu(values):
    return 0.5 * values * (1.0 + lax.erf(values * 0.7071067811865476))


def at_place(spot):
    spot = (spot + 2 * SEQ) % SEQ
    upper = spot // (SEQ // 2)
    return (1 - upper) * 2 * spot + upper * (2 * (SEQ - 1 - spot) + 1)


def tower_kernel(
    x_ref,
    gain_ref,
    conv_ref,
    conv_bias_ref,
    point_ref,
    point_bias_ref,
    head_ref,
    head_bias_ref,
    start_ref,
    length_ref,
    owner_ref,
    slot_ref,
    out_ref,
    pack_conv,
    pack_head,
    conv_w,
    point_w,
    head_w,
    small,
    inbox,
    outbox,
    past,
    past_x,
    act,
    hid,
    counts,
    conv_bias,
    point_bias,
    head_bias,
    finals,
    total,
    landed,
    w_send,
    w_recv,
    f_send,
    h_send,
    h_recv,
    g_send,
    g_recv,
    s_send,
    s_recv,
    x_send,
    x_recv,
    c_send,
    t_send,
    t_recv,
):
    seq = lax.axis_index("seq")
    ch = lax.axis_index("ch")
    odd = seq % 2
    place = (1 - odd) * (seq // 2) + odd * (SEQ - 1 - seq // 2)
    stage = (place - START + SEQ) % SEQ
    sibling = ch + 1 - 2 * (ch % 2)
    across = (ch + 2) % CHS
    diagonal = (sibling + 2) % CHS
    first_seq = at_place(START)
    rows, width = x_ref.shape
    chans = width * CHS
    depth = conv_ref.shape[2]
    lines = point_ref.shape[1]

    barrier = pltpu.get_barrier_semaphore()

    @pl.loop(1, SEQ * CHS)
    def _(step):
        peer = (seq * CHS + ch + step) % (SEQ * CHS)
        pl.semaphore_signal(
            barrier, inc=1, device_id=(peer // CHS, peer % CHS), device_id_type=MESH
        )

    def remote(src, dst, send, recv, target):
        return pltpu.make_async_remote_copy(
            src_ref=src,
            dst_ref=dst,
            send_sem=send,
            recv_sem=recv,
            device_id=target,
            device_id_type=MESH,
        )

    def conv_spot(origin, block):
        return conv_w.at[
            pl.ds(pl.multiple_of(origin * depth, 64), depth),
            pl.ds(pl.multiple_of(block * CONV, 128), CONV),
        ]

    def point_spot(origin, block):
        row = (origin // 2) * WIDE + (origin % 2) * lines
        return point_w.at[
            pl.ds(pl.multiple_of(row, 32), lines),
            pl.ds(pl.multiple_of(block * width, 128), width),
        ]

    def head_spot(origin):
        return head_w.at[pl.ds(pl.multiple_of(origin * depth, 64), depth)]

    def pack(layer):
        taps = [conv_ref[layer, tap] for tap in range(3)]
        own = pack_conv.at[layer]
        own[:, 0:128] = taps[0][:, 0:128]
        own[:, 128:256] = taps[1][:, 0:128]
        own[:, 256:384] = jnp.concatenate([taps[0][:, 128:192], taps[1][:, 128:192]], axis=1)
        own[:, 384:512] = taps[2][:, 0:128]
        own[:, 512:640] = jnp.concatenate(
            [taps[2][:, 128:192], jnp.zeros((depth, 64), jnp.bfloat16)], axis=1
        )

    def layer_copies(layer, peer, number):
        target = (at_place(layer + START), peer)
        return (
            remote(
                pack_conv.at[layer],
                conv_spot(seq, ch),
                w_send.at[number, layer, 0],
                w_recv.at[number, seq, 0],
                target,
            ),
            remote(
                point_ref.at[layer],
                point_spot(seq, ch),
                w_send.at[number, layer, 1],
                w_recv.at[number, seq, 1],
                target,
            ),
        )

    def own_layer():
        return (
            pltpu.make_async_copy(
                pack_conv.at[stage], conv_spot(seq, ch), w_recv.at[0, seq, 0]
            ),
            pltpu.make_async_copy(
                point_ref.at[stage], point_spot(seq, ch), w_recv.at[0, seq, 1]
            ),
        )

    def each_layer(act_on):
        for offset in OFFSETS[1:]:
            layer = (stage + offset + SEQ) % SEQ
            act_on(layer, layer_copies(layer, ch, 0))

            @pl.when(layer < BOTH)
            def _():
                act_on(None, layer_copies(layer, across, 1))

    def start_layer(layer, copies):
        if layer is not None:
            pack(layer)
        for copy in copies:
            copy.start()

    def finish_layer(layer, copies):
        for copy in copies:
            copy.wait_send()

    def head_copy():
        return remote(pack_head, head_spot(seq), h_send, h_recv.at[seq], (first_seq, ch))

    def own_head():
        return pltpu.make_async_copy(pack_head, head_spot(seq), h_recv.at[seq])

    def stream_sends(act_on):
        parts = rows // TILE
        for dest in range(CHS):
            for part in range(parts):
                chunk = seq * parts + part - (STEP // TILE) * dest
                inside = (chunk >= 0) & (chunk < CHUNKS)
                chunk_at = jnp.clip(chunk, 0, CHUNKS - 1)
                mine = (seq == first_seq) & (ch == dest)
                src = x_ref.at[pl.ds(part * TILE, TILE)]
                dst = inbox.at[
                    chunk_at, :, pl.ds(pl.multiple_of(ch * width, 128), width)
                ]
                act_on(dest, part, inside, mine, chunk_at, src, dst)

    def start_early(dest, part, inside, *rest):
        start_stream(dest, part, inside & (rest[1] < EARLY), *rest)

    def start_late(dest, part, inside, *rest):
        start_stream(dest, part, inside & (rest[1] >= EARLY), *rest)

    def start_stream(dest, part, inside, mine, chunk, src, dst):
        @pl.when(inside & mine)
        def _():
            pltpu.make_async_copy(src, dst, x_recv.at[chunk]).start()

        @pl.when(inside & jnp.logical_not(mine))
        def _():
            remote(
                src, dst, c_send.at[dest, part], x_recv.at[chunk], (first_seq, dest)
            ).start()

    def finish_stream(dest, part, inside, mine, chunk, src, dst):
        @pl.when(inside & jnp.logical_not(mine))
        def _():
            remote(
                src, dst, c_send.at[dest, part], x_recv.at[chunk], (first_seq, dest)
            ).wait_send()

    pack(stage)
    own_small = small.at[ch]
    own_small[...] = jnp.zeros(own_small.shape, jnp.float32)
    own_small[0:LAYERS, 0 : conv_bias_ref.shape[1]] = conv_bias_ref[...]
    own_small[0:LAYERS, WIDE : WIDE + width] = point_bias_ref[...]
    head_bias[...] = jnp.zeros_like(head_bias)
    head_bias[:, 0 : head_bias_ref.shape[1]] = head_bias_ref[...]
    used = 2 * lines
    for block in range(CHS):
        point_w[block * WIDE + used : (block + 1) * WIDE, :] = jnp.zeros(
            (WIDE - used, chans), jnp.bfloat16
        )
    pl.semaphore_wait(barrier, SEQ * CHS - 1)

    for copy in own_layer():
        copy.start()
    small_copies = [
        remote(
            small.at[ch], small.at[ch], s_send.at[number], s_recv.at[number], (seq, peer)
        )
        for number, peer in enumerate((across, sibling, diagonal))
    ]
    for copy in small_copies:
        copy.start()
    stream_sends(start_early)
    each_layer(start_layer)
    tracks = head_ref.shape[1]
    edge = tracks // 128 * 128
    pack_head[:, edge:] = jnp.zeros((depth, HEADW - edge), jnp.bfloat16)
    pack_head[:, 0:tracks] = head_ref[...]

    @pl.when(seq == first_seq)
    def _():
        own_head().start()

    @pl.when(seq != first_seq)
    def _():
        head_copy().start()

    past[0:256, :] = jnp.zeros((256, past.shape[1]), jnp.float32)
    past_x[0:128, :] = jnp.zeros((128, chans), jnp.float32)

    @pl.when(seq == first_seq)
    def _():
        slots = slot_ref.shape[1]

        @pl.when(ch == CHS - 1)
        def _():
            for chunk in range((SEQ * rows - STEP * (CHS - 1)) // TILE, CHUNKS):
                inbox[chunk] = jnp.zeros((TILE, chans), jnp.bfloat16)

        @pl.loop(0, GROUPS - IDLE)
        def _(group):
            place_in = lax.broadcasted_iota(
                jnp.int32, (CHS * GROUP, start_ref.shape[1]), 0
            )
            quarter = place_in // GROUP
            local_row = (group + IDLE) * GROUP + place_in % GROUP
            bins = quarter * STEP + local_row - (2**LAYERS - 1)
            least = 255 + 256 * jnp.minimum(quarter, 1)
            owned_bin = (local_row >= least) & (local_row < GROUPS * GROUP - 1)
            member = (
                (bins >= start_ref[...])
                & (bins < start_ref[...] + length_ref[...])
                & owned_bin
            )
            names = lax.broadcasted_iota(jnp.int32, (slots, owner_ref.shape[1]), 0)
            owned = lax.dot_general(
                jnp.where(names == owner_ref[...], 1.0, 0.0).astype(jnp.bfloat16),
                jnp.where(member, 1.0, 0.0).astype(jnp.bfloat16),
                (((1,), (1,)), ((), ())),
                preferred_element_type=jnp.float32,
            )
            order = lax.broadcasted_iota(jnp.int32, (slots, slots), 0) == slot_ref[...]
            counts[group] = jnp.dot(
                jnp.where(order, 1.0, 0.0).astype(jnp.bfloat16),
                owned.astype(jnp.bfloat16),
                preferred_element_type=jnp.float32,
            ).astype(jnp.bfloat16)

    def arrive(number, origin):
        block = (ch, across, sibling, diagonal)[number]
        for part, spot in ((0, conv_spot(origin, block)), (1, point_spot(origin, block))):
            remote(
                spot, spot, f_send.at[0, 0, 0], w_recv.at[number, origin, part], (seq, sibling)
            ).wait_recv()

    def forward(number, origin, kind):
        block = (ch, across)[number]
        peer, arrival = ((across, 1), (sibling, 2), (sibling, 3))[kind]
        return [
            remote(
                spot,
                spot,
                f_send.at[kind, origin, part],
                w_recv.at[arrival, origin, part],
                (seq, peer),
            )
            for part, spot in (
                (0, conv_spot(origin, block)),
                (1, point_spot(origin, block)),
            )
        ]

    def across_too(origin):
        return (stage >= BOTH) | (origin == seq)

    def take_direct(origin):
        arrive(0, origin)

        @pl.when(across_too(origin))
        def _():
            for copy in forward(0, origin, 0):
                copy.start()

        for copy in forward(0, origin, 1):
            copy.start()

    def take_across(origin):
        arrive(1, origin)
        for copy in forward(1, origin, 2):
            copy.start()

    origins = [at_place(place + offset) for offset in OFFSETS]
    for number, origin in enumerate(origins):
        take_direct(origin)
        if number:
            take_across(origins[number - 1])
    take_across(origins[-1])
    for copy in small_copies:
        copy.wait_recv()
    for block in range(CHS):
        conv_bias[:, block * WIDE : (block + 1) * WIDE] = small[block, pl.ds(stage, 1), 0:WIDE]
        point_bias[:, block * width : (block + 1) * width] = small[
            block, pl.ds(stage, 1), WIDE : WIDE + width
        ]
    for origin in origins:
        arrive(2, origin)
        arrive(3, origin)
    stream_sends(start_late)


    spread = 1
    for number in range(1, SEQ):
        spread = spread + (2 ** (number - 1)) * jnp.where(stage >= number, 1, 0)
    after = at_place(place + 1)

    def norm_rows(slot, turn, first, count):
        wide = inbox[slot, pl.ds(first, count), :].astype(jnp.float32)
        squares = jnp.sum(wide * wide, axis=1, keepdims=True)
        scale = lax.rsqrt(squares / chans + 1e-06)
        return wide, wide * scale * gain_ref[pl.ds(turn, 1), :]

    def hop(chunk):
        landing = chunk + CHUNKS * jnp.where(stage == SEQ - 1, 1, 0)
        return remote(
            outbox.at[chunk], inbox.at[landing], x_send.at[chunk], x_recv.at[landing], (after, ch)
        )

    def inbox_arrive(slot):
        remote(
            inbox.at[slot], inbox.at[slot], x_send.at[0], x_recv.at[slot], (after, ch)
        ).wait_recv()

    sub = 16

    def shifted(ref, base, lag, lanes):
        steps = (lag + 7) // 8
        window = ref[pl.ds(pl.multiple_of(base - steps * 8, 8), TILE + 8), lanes]
        turn = (TILE + 8 - steps * 8 + lag) % (TILE + 8)
        return pltpu.roll(window, turn, 0)[0:TILE]

    def run_chunk(chunk):
        base = pl.multiple_of(chunk * TILE, TILE)

        absent = (seq == first_seq) & (
            ch * STEP + chunk * TILE >= SEQ * rows
        )

        @pl.when(jnp.logical_not(absent))
        def _():
            inbox_arrive(chunk)

        for first in range(0, TILE, sub):
            wide, normed = norm_rows(chunk, stage, first, sub)
            bins = (
                ch * STEP
                + chunk * TILE
                + first
                - (spread - 1)
                + lax.broadcasted_iota(jnp.int32, (sub, chans), 0)
            )
            inside = (bins >= 0) & (bins < SEQ * rows)
            act[first : first + sub, :] = jnp.where(inside, gelu(normed), 0.0).astype(
                jnp.bfloat16
            )
            past_x[pl.ds(128 + base + first, sub), :] = wide
        for block in range(CHS):
            taps = jnp.dot(
                act[...],
                conv_w[:, block * CONV : (block + 1) * CONV],
                preferred_element_type=jnp.float32,
            )
            lane = block * KEPT
            past[pl.ds(256 + base, TILE), lane : lane + KEPT] = taps[:, 0:KEPT]
            far, near = 2 * spread, spread
            left = (
                shifted(past, 256 + base, far, slice(lane, lane + 128))
                + shifted(past, 256 + base, near, slice(lane + 128, lane + 256))
                + taps[:, KEPT : KEPT + 128]
                + conv_bias[:, block * WIDE : block * WIDE + 128]
            )
            right = (
                shifted(past, 256 + base, far, slice(lane + 256, lane + 384))
                + pltpu.roll(shifted(past, 256 + base, near, slice(lane + 256, lane + 384)), 64, 1)
                + taps[:, KEPT + 128 : CONV]
                + conv_bias[:, block * WIDE + 128 : (block + 1) * WIDE]
            )
            hid[:, block * WIDE : block * WIDE + 128] = gelu(left).astype(jnp.bfloat16)
            hid[:, block * WIDE + 128 : (block + 1) * WIDE] = gelu(right).astype(jnp.bfloat16)
        for block in range(CHS):
            lanes = slice(block * width, (block + 1) * width)
            mixed = jnp.dot(hid[...], point_w[:, lanes], preferred_element_type=jnp.float32)
            outbox[chunk, :, lanes] = (
                shifted(past_x, 128 + base, spread, lanes) + mixed + point_bias[:, lanes]
            ).astype(jnp.bfloat16)
        hop(chunk).start()

    @pl.loop(0, CHUNKS)
    def _(chunk):
        run_chunk(chunk)

    def total_copy(origin):
        return remote(
            total.at[pl.ds(origin * 8, 8)],
            landed,
            t_send.at[origin],
            t_recv,
            (origin, ch),
        )

    def final_copies(group):
        def copy(block, peer, number):
            return remote(
                finals.at[group, block],
                finals.at[group, block],
                g_send.at[number, group],
                g_recv.at[number, group],
                (seq, peer),
            )

        return copy(ch, across, 0), copy(ch, sibling, 1), copy(across, sibling, 2)

    def give_group(group):
        for part in range(GROUP // TILE):
            slot = CHUNKS + (group + IDLE) * (GROUP // TILE) + part
            inbox_arrive(slot)
            for first in range(0, TILE, sub):
                _, normed = norm_rows(slot, LAYERS, first, sub)
                start = part * TILE + first
                finals[group, ch, start : start + sub, :] = normed.astype(jnp.bfloat16)
        to_across, to_sibling, _ = final_copies(group)
        to_across.start()
        to_sibling.start()

    def take_group(group):
        to_across, to_sibling, onward = final_copies(group)
        to_across.wait_recv()
        onward.start()
        to_sibling.wait_recv()
        onward.wait_recv()
        rows_in = finals[group].reshape(CHS * GROUP, chans)
        for start in range(0, HEADW, 256):
            lanes = slice(start, start + 256)
            logits = (
                jnp.dot(rows_in, head_w[:, lanes], preferred_element_type=jnp.float32)
                + head_bias[:, lanes]
            )
            cover = jnp.maximum(logits, 0.0) + jnp.log1p(jnp.exp(-jnp.abs(logits)))
            sums = total[:, lanes]
            for _ in range(3):
                piece = cover.astype(jnp.bfloat16)
                sums = sums + jnp.dot(
                    counts[group], piece, preferred_element_type=jnp.float32
                )
                cover = cover - piece.astype(jnp.float32)
            total[:, lanes] = sums

    @pl.when(seq == first_seq)
    def _():
        for origin in origins:
            head_copy_in = remote(
                pack_head, head_spot(origin), h_send, h_recv.at[origin], (seq, sibling)
            )
            head_copy_in.wait_recv()
        total[...] = jnp.zeros_like(total)

        @pl.loop(0, IDLE * GROUP // TILE)
        def _(chunk):
            inbox_arrive(CHUNKS + chunk)

        give_group(0)

        @pl.loop(1, GROUPS - IDLE)
        def _(group):
            give_group(group)
            take_group(group - 1)

        take_group(GROUPS - IDLE - 1)
        for origin in range(SEQ):

            @pl.when(origin == first_seq)
            def _():
                pltpu.make_async_copy(total.at[pl.ds(origin * 8, 8)], landed, t_recv).start()

            @pl.when(origin != first_seq)
            def _():
                total_copy(origin).start()

    each_layer(finish_layer)

    @pl.when(seq != first_seq)
    def _():
        head_copy().wait_send()

    stream_sends(finish_stream)
    for copy in small_copies:
        copy.wait_send()
    for origin in origins:

        @pl.when(across_too(origin))
        def _():
            for copy in forward(0, origin, 0):
                copy.wait_send()

        for copy in forward(0, origin, 1) + forward(1, origin, 2):
            copy.wait_send()

    @pl.loop(0, CHUNKS)
    def _(chunk):
        hop(chunk).wait_send()

    remote(landed, landed, t_send.at[0], t_recv, (seq, sibling)).wait_recv()
    out_ref[...] = jnp.log1p(landed[...])[:, : out_ref.shape[1]]

    @pl.when(seq == first_seq)
    def _():
        @pl.loop(0, GROUPS - IDLE)
        def _(group):
            for copy in final_copies(group):
                copy.wait_send()

        for origin in range(SEQ):

            @pl.when(origin != first_seq)
            def _():
                total_copy(origin).wait_send()


def local_kernel(
    stream,
    norm_gain,
    conv_weight,
    conv_bias,
    point_weight,
    point_bias,
    head_weight,
    head_bias,
    exon_start,
    exon_length,
    exon_transcript,
    transcript_slot,
):
    rows, width = stream.shape
    depth = conv_weight.shape[2]
    tracks = head_weight.shape[1]
    slots = transcript_slot.shape[0]
    chans = CHS * width
    vmem = pl.BlockSpec(memory_space=pltpu.VMEM)
    dma = pltpu.SemaphoreType.DMA
    f32, bf16 = jnp.float32, jnp.bfloat16
    return pl.pallas_call(
        tower_kernel,
        out_shape=jax.ShapeDtypeStruct((slots // SEQ, tracks), f32),
        in_specs=[vmem] * 12,
        out_specs=vmem,
        scratch_shapes=[
            pltpu.VMEM((LAYERS, depth, CONV), bf16),
            pltpu.VMEM((depth, HEADW), bf16),
            pltpu.VMEM((chans, CHS * CONV), bf16),
            pltpu.VMEM((CHS * WIDE, chans), bf16),
            pltpu.VMEM((chans, HEADW), bf16),
            pltpu.VMEM((CHS, 8, 640), f32),
            pltpu.VMEM((2 * CHUNKS, TILE, chans), bf16),
            pltpu.VMEM((CHUNKS, TILE, chans), bf16),
            pltpu.VMEM((264 + CHUNKS * TILE, CHS * KEPT), f32),
            pltpu.VMEM((136 + CHUNKS * TILE, chans), f32),
            pltpu.VMEM((TILE, chans), bf16),
            pltpu.VMEM((TILE, CHS * WIDE), bf16),
            pltpu.VMEM((GROUPS - IDLE, slots, CHS * GROUP), bf16),
            pltpu.VMEM((1, CHS * WIDE), f32),
            pltpu.VMEM((1, chans), f32),
            pltpu.VMEM((1, HEADW), f32),
            pltpu.VMEM((GROUPS - IDLE, CHS, GROUP, chans), bf16),
            pltpu.VMEM((slots, HEADW), f32),
            pltpu.VMEM((slots // SEQ, HEADW), f32),
            dma((2, LAYERS, 2)),
            dma((4, SEQ, 2)),
            dma((3, SEQ, 2)),
            dma(()),
            dma((SEQ,)),
            dma((3, GROUPS - IDLE)),
            dma((3, GROUPS - IDLE)),
            dma((3,)),
            dma((3,)),
            dma((CHUNKS,)),
            dma((2 * CHUNKS,)),
            dma((CHS, rows // TILE)),
            dma((SEQ,)),
            dma(()),
        ],
        compiler_params=pltpu.CompilerParams(
            collective_id=0, has_side_effects=True, vmem_limit_bytes=60 * 2**20
        ),
        cost_estimate=pl.CostEstimate(
            flops=20_000_000_000, bytes_accessed=4_000_000, transcendentals=8_000_000
        ),
    )(
        stream,
        norm_gain,
        conv_weight,
        conv_bias,
        point_weight,
        point_bias,
        head_weight,
        head_bias[None, :],
        exon_start[None, :],
        exon_length[None, :],
        exon_transcript[None, :],
        transcript_slot[None, :],
    )


def local(*args):
    stream, conv_weight, point_weight, head_weight = args[0], args[2], args[4], args[6]
    fits = (
        lax.axis_size("seq") == SEQ
        and lax.axis_size("ch") == CHS
        and stream.shape == (256, 384)
        and conv_weight.shape[1:] == (3, 192, 192)
        and point_weight.shape[1:] == (96, 384)
        and head_weight.shape == (192, 960)
        and args[11].shape[0] == 8 * SEQ
    )
    return local_kernel(*args) if fits else local_plain(*args)


def solution(mesh):
    placed = (
        P("seq", "ch"),
        P(),
        P(None, None, "seq", "ch"),
        P(None, "ch"),
        P(None, "seq", "ch"),
        P(None, "ch"),
        P("seq", "ch"),
        P("ch"),
        P(),
        P(),
        P(),
        P(),
    )
    return jax.shard_map(
        local, mesh=mesh, in_specs=placed, out_specs=P("seq", "ch"), check_vma=False
    )
```

time: 256 us -> 229 us (0.89)
  Pallas kernels: 254 us -> 228 us
    pallas_call x1, Pallas kernels: 254 us -> 228 us  [local_kernel(): pl.pallas_call(tower_kernel, out_shape=jax.ShapeDtypeStruct((slots // SEQ...]
where the time goes in v1:
time: 229 us
  Pallas kernels  228 us (100%)
    pallas_call x1, Pallas kernels, local_kernel(): pl.pallas_call(tower_kernel, out_shape=jax.ShapeDtypeStruct((slots // SEQ...  228 us

profile of v1, /device:TPU:0, one launch (start us, length us, event | category | flops | bytes accessed | tf_op | source)
XLA Modules:
  0.0 228.9 jit_solution(2749790723051818628)
XLA Ops:
  0.0 227.6 %shard_map.118 = f32[8,960]{1,0:T(8,128)} custom-call(bf16[256,384]{1,0:T(8,128)(2,1)} %x_ref.1, f32[9,1536]{1,0:T(8,128)} %gain_ref.1, bf16[8,3,192,192]{3,2,1,0:T(8,128)(2,1)} %conv_ref.1, f32[8,192]{1,0:T(8,128)} %conv_bias_ref.1, bf16[8,96,384]{2,1,0:T(8,128)(2,1)} %point_ref.1, f32[8,384]{1,0:T(8,128)} %point_bias_ref.1, bf16[192,960]{1,0:T(8,128)(2,1)} %head_ref.1, ...), custom_call_target="tpu_custom_call" | custom-call | flops 20000000000 | bytes 4000000 | tf_op jit(solution)/shard_map/pallas_call | solution.py:714
  227.6 1.4 copy.14

commit v2 on v1

--- a/solution.py
+++ b/solution.py
@@ -107,9 +107,9 @@
 START = 2
 TILE = 32
 CHUNKS = 960 // TILE
-GROUP = 64
+GROUP = 96
 GROUPS = 960 // GROUP
-IDLE = 3
+IDLE = 2
 EARLY = 192 // TILE
 STEP = 448
 CONV = 640
@@ -175,6 +175,7 @@
     x_send,
     x_recv,
     c_send,
+    e_send,
     t_send,
     t_recv,
 ):
@@ -297,7 +298,7 @@
         for dest in range(CHS):
             for part in range(parts):
                 chunk = seq * parts + part - (STEP // TILE) * dest
-                inside = (chunk >= 0) & (chunk < CHUNKS)
+                inside = (chunk >= 0) & (chunk < (CHUNKS if dest % 2 else STEP // TILE))
                 chunk_at = jnp.clip(chunk, 0, CHUNKS - 1)
                 mine = (seq == first_seq) & (ch == dest)
                 src = x_ref.at[pl.ds(part * TILE, TILE)]
@@ -496,6 +497,17 @@
 
     sub = 16
 
+    def pass_stream(chunk):
+        return remote(
+            inbox.at[chunk],
+            inbox.at[chunk + STEP // TILE],
+            e_send.at[chunk],
+            x_recv.at[chunk + STEP // TILE],
+            (seq, sibling),
+        )
+
+    passing = (seq == first_seq) & (ch % 2 == 1)
+
     def shifted(ref, base, lag, lanes):
         steps = (lag + 7) // 8
         window = ref[pl.ds(pl.multiple_of(base - steps * 8, 8), TILE + 8), lanes]
@@ -512,6 +524,10 @@
         @pl.when(jnp.logical_not(absent))
         def _():
             inbox_arrive(chunk)
+
+        @pl.when(passing & (chunk < CHUNKS - STEP // TILE))
+        def _():
+            pass_stream(chunk).start()
 
         for first in range(0, TILE, sub):
             wide, normed = norm_rows(chunk, stage, first, sub)
@@ -583,10 +599,17 @@
 
         return copy(ch, across, 0), copy(ch, sibling, 1), copy(across, sibling, 2)
 
-    def give_group(group):
+    def pass_on(group):
+        to_across, _, onward = final_copies(group)
+        to_across.wait_recv()
+        onward.start()
+
+    def give_group(group, between=None):
         for part in range(GROUP // TILE):
             slot = CHUNKS + (group + IDLE) * (GROUP // TILE) + part
             inbox_arrive(slot)
+            if part == 0 and between is not None:
+                between()
             for first in range(0, TILE, sub):
                 _, normed = norm_rows(slot, LAYERS, first, sub)
                 start = part * TILE + first
@@ -596,9 +619,7 @@
         to_sibling.start()
 
     def take_group(group):
-        to_across, to_sibling, onward = final_copies(group)
-        to_across.wait_recv()
-        onward.start()
+        _, to_sibling, onward = final_copies(group)
         to_sibling.wait_recv()
         onward.wait_recv()
         rows_in = finals[group].reshape(CHS * GROUP, chans)
@@ -635,9 +656,10 @@
 
         @pl.loop(1, GROUPS - IDLE)
         def _(group):
-            give_group(group)
+            give_group(group, lambda: pass_on(group - 1))
             take_group(group - 1)
 
+        pass_on(GROUPS - IDLE - 1)
         take_group(GROUPS - IDLE - 1)
         for origin in range(SEQ):
 
@@ -671,6 +693,10 @@
     @pl.loop(0, CHUNKS)
     def _(chunk):
         hop(chunk).wait_send()
+
+        @pl.when(passing & (chunk < CHUNKS - STEP // TILE))
+        def _():
+            pass_stream(chunk).wait_send()
 
     remote(landed, landed, t_send.at[0], t_recv, (seq, sibling)).wait_recv()
     out_ref[...] = jnp.log1p(landed[...])[:, : out_ref.shape[1]]
@@ -748,6 +774,7 @@
             dma((CHUNKS,)),
             dma((2 * CHUNKS,)),
             dma((CHS, rows // TILE)),
+            dma((CHUNKS - STEP // TILE,)),
             dma((SEQ,)),
             dma(()),
         ],

time: 229 us -> 225 us (0.983)
  Pallas kernels: 228 us -> 223 us
    pallas_call x1, Pallas kernels: 228 us -> 223 us  [local_kernel(): pl.pallas_call(tower_kernel, out_shape=jax.ShapeDtypeStruct((slots // SEQ...]
where the time goes in v2:
time: 225 us; the launch traced here: 224 us
  Pallas kernels  223 us (99%)
    pallas_call x1, Pallas kernels, local_kernel(): pl.pallas_call(tower_kernel, out_shape=jax.ShapeDtypeStruct((slots // SEQ...  223 us

profile of v2, /device:TPU:0, one launch (start us, length us, event | category | flops | bytes accessed | tf_op | source)
XLA Modules:
  0.0 224.0 jit_solution(7033370882257466220)
XLA Ops:
  0.0 222.6 %shard_map.118 = f32[8,960]{1,0:T(8,128)} custom-call(bf16[256,384]{1,0:T(8,128)(2,1)} %x_ref.1, f32[9,1536]{1,0:T(8,128)} %gain_ref.1, bf16[8,3,192,192]{3,2,1,0:T(8,128)(2,1)} %conv_ref.1, f32[8,192]{1,0:T(8,128)} %conv_bias_ref.1, bf16[8,96,384]{2,1,0:T(8,128)(2,1)} %point_ref.1, f32[8,384]{1,0:T(8,128)} %point_bias_ref.1, bf16[192,960]{1,0:T(8,128)(2,1)} %head_ref.1, ...), custom_call_target="tpu_custom_call" | custom-call | flops 20000000000 | bytes 4000000 | tf_op jit(solution)/shard_map/pallas_call | solution.py:740
  222.6 1.4 copy.14

commit v3 on v2

--- a/solution.py
+++ b/solution.py
@@ -107,9 +107,10 @@
 START = 2
 TILE = 32
 CHUNKS = 960 // TILE
-GROUP = 96
+GROUP = 160
 GROUPS = 960 // GROUP
-IDLE = 2
+IDLE = 1
+LATE = 511 // GROUP - IDLE
 EARLY = 192 // TILE
 STEP = 448
 CONV = 640
@@ -382,6 +383,10 @@
             for chunk in range((SEQ * rows - STEP * (CHS - 1)) // TILE, CHUNKS):
                 inbox[chunk] = jnp.zeros((TILE, chans), jnp.bfloat16)
 
+        for group in range(LATE):
+            for block in range(1, CHS):
+                finals[group, block] = jnp.zeros((GROUP, chans), jnp.bfloat16)
+
         @pl.loop(0, GROUPS - IDLE)
         def _(group):
             place_in = lax.broadcasted_iota(
@@ -599,10 +604,16 @@
 
         return copy(ch, across, 0), copy(ch, sibling, 1), copy(across, sibling, 2)
 
+    def needed(block, group):
+        return (block == 0) | (group >= LATE)
+
     def pass_on(group):
         to_across, _, onward = final_copies(group)
-        to_across.wait_recv()
-        onward.start()
+
+        @pl.when(needed(across, group))
+        def _():
+            to_across.wait_recv()
+            onward.start()
 
     def give_group(group, between=None):
         for part in range(GROUP // TILE):
@@ -615,13 +626,23 @@
                 start = part * TILE + first
                 finals[group, ch, start : start + sub, :] = normed.astype(jnp.bfloat16)
         to_across, to_sibling, _ = final_copies(group)
-        to_across.start()
-        to_sibling.start()
+
+        @pl.when(needed(ch, group))
+        def _():
+            to_across.start()
+            to_sibling.start()
 
     def take_group(group):
         _, to_sibling, onward = final_copies(group)
-        to_sibling.wait_recv()
-        onward.wait_recv()
+
+        @pl.when(needed(sibling, group))
+        def _():
+            to_sibling.wait_recv()
+
+        @pl.when(needed(diagonal, group))
+        def _():
+            onward.wait_recv()
+
         rows_in = finals[group].reshape(CHS * GROUP, chans)
         for start in range(0, HEADW, 256):
             lanes = slice(start, start + 256)
@@ -705,8 +726,16 @@
     def _():
         @pl.loop(0, GROUPS - IDLE)
         def _(group):
-            for copy in final_copies(group):
-                copy.wait_send()
+            to_across, to_sibling, onward = final_copies(group)
+
+            @pl.when(needed(ch, group))
+            def _():
+                to_across.wait_send()
+                to_sibling.wait_send()
+
+            @pl.when(needed(across, group))
+            def _():
+                onward.wait_send()
 
         for origin in range(SEQ):
 

time: 225 us -> 223 us (level)
  no operation moved by 1% of the time
where the time goes in v3:
time: 223 us; the launch traced here: 222 us
  Pallas kernels  221 us (99%)
    pallas_call x1, Pallas kernels, local_kernel(): pl.pallas_call(tower_kernel, out_shape=jax.ShapeDtypeStruct((slots // SEQ...  221 us

profile of v3, /device:TPU:0, one launch (start us, length us, event | category | flops | bytes accessed | tf_op | source)
XLA Modules:
  0.0 222.1 jit_solution(13790997658576232108)
XLA Ops:
  0.0 220.7 %shard_map.118 = f32[8,960]{1,0:T(8,128)} custom-call(bf16[256,384]{1,0:T(8,128)(2,1)} %x_ref.1, f32[9,1536]{1,0:T(8,128)} %gain_ref.1, bf16[8,3,192,192]{3,2,1,0:T(8,128)(2,1)} %conv_ref.1, f32[8,192]{1,0:T(8,128)} %conv_bias_ref.1, bf16[8,96,384]{2,1,0:T(8,128)(2,1)} %point_ref.1, f32[8,384]{1,0:T(8,128)} %point_bias_ref.1, bf16[192,960]{1,0:T(8,128)(2,1)} %head_ref.1, ...), custom_call_target="tpu_custom_call" | custom-call | flops 20000000000 | bytes 4000000 | tf_op jit(solution)/shard_map/pallas_call | solution.py:769
  220.7 1.4 copy.14
